TPU v7x, 128 devices: a whole 4x4x4 slice. The times are simulated.
128 devices in a mesh: row: 16 (over y, z_hi, core), col: 8 (over x, z_lo).
Axes of the slice: x: 4, y: 4, z: 4 (z_hi: 2, z_lo: 2; z = z_hi * 2 + z_lo), core: 2. Of those that a mesh axis runs over, the one named last changes fastest.
Arguments:
- pair: bfloat16 [640, 640, 128], P('row', 'col'), may hold values from -6 to 6
- pair_mask: int32 [640, 640], P('row', 'col'), may hold values 0 or 1
- norm_gain: float32 [128], replicated, may hold values from 0.1 to 1.9
- norm_bias: float32 [128], replicated, may hold values from -3 to 3
- proj_weight: bfloat16 [128, 256], replicated, may hold values from -0.5 to 0.5
- gate_weight: bfloat16 [128, 256], replicated, may hold values from -0.5 to 0.5
- out_gain: float32 [128], replicated, may hold values from 0.1 to 1.9
- out_bias: float32 [128], replicated, may hold values from -3 to 3
- out_weight: bfloat16 [128, 128], replicated, may hold values from -0.5 to 0.5
- out_gate_weight: bfloat16 [128, 128], replicated, may hold values from -0.5 to 0.5
Outputs:
- update: bfloat16 [640, 640, 128], P('row', 'col')
All inputs are finite; a program needn't handle non-finite values. No bound on the sum of `pair_mask` on one device may be relied on, other than what follows from the above.
Results may differ from a plain program's by a relative error of at most 0.015.
Values may be sent and summed in bfloat16 or wider, within the bound.
A program may use at most 128 MiB of HBM per device.

v0:
```python
import jax
import jax.numpy as jnp
from jax import lax
from jax.sharding import PartitionSpec as P


def layer_norm(values, gain, bias):
    mean = jnp.mean(values, axis=-1, keepdims=True)
    centred = values - mean
    var = jnp.mean(centred * centred, axis=-1, keepdims=True)
    return centred * lax.rsqrt(var + 1e-05) * gain + bias


def body(
    pair,
    pair_mask,
    norm_gain,
    norm_bias,
    proj_weight,
    gate_weight,
    out_gain,
    out_bias,
    out_weight,
    out_gate_weight,
):
    hidden = proj_weight.shape[1] // 2
    normed = layer_norm(pair.astype(jnp.float32), norm_gain, norm_bias).astype(jnp.bfloat16)
    proj = jnp.dot(normed, proj_weight, preferred_element_type=jnp.float32)
    gate = jnp.dot(normed, gate_weight, preferred_element_type=jnp.float32)
    packed = (proj * jax.nn.sigmoid(gate) * pair_mask[..., None].astype(jnp.float32)).astype(
        jnp.bfloat16
    )
    left = packed[..., :hidden]
    right = packed[..., hidden:]
    right_all = lax.all_gather(right, "row", axis=0, tiled=True)
    right_mine = lax.all_to_all(right_all, "col", split_axis=0, concat_axis=1, tiled=True)
    width = left.shape[1]
    piece = lax.all_gather(left, "col", axis=1, tiled=True)
    count = piece.shape[1] // width
    left_parts = piece.reshape(piece.shape[0], count, width, hidden)
    right_parts = right_mine.reshape(right_mine.shape[0], count, width, hidden)
    partial_value = jnp.einsum(
        "ibkd,jbkd->bijd", left_parts, right_parts, preferred_element_type=jnp.float32
    )
    rounded = lax.optimization_barrier(partial_value.astype(jnp.bfloat16))
    combined = jnp.sum(rounded.astype(jnp.float32), axis=0)
    finished = layer_norm(combined, out_gain, out_bias).astype(jnp.bfloat16)
    projected = jnp.dot(finished, out_weight, preferred_element_type=jnp.float32)
    gating = jax.nn.sigmoid(jnp.dot(normed, out_gate_weight, preferred_element_type=jnp.float32))
    return (projected * gating).astype(jnp.bfloat16)


def solution(mesh):
    placed = (P("row", "col", None), P("row", "col"), P(), P(), P(), P(), P(), P(), P(), P())
    return jax.shard_map(
        body, mesh=mesh, in_specs=placed, out_specs=P("row", "col", None), check_vma=False
    )
```

profile of v0, /device:TPU:1, one launch (start us, length us, event | category | flops | bytes accessed | tf_op | source)
XLA Modules:
  0.0 461.7 jit_solution(5204431303035232350)
XLA Ops:
  6.5 0.0 all-gather.3.cloned.1.call-start
  6.6 1.6 convert_reduce_fusion.2
  8.2 2.3 fusion.6
  10.7 0.0 copy-start.9
  10.7 1.0 fusion.11
  11.7 1.8 multiply_convert_fusion
  13.5 1.5 fusion.20
  15.0 0.0 all-gather.3.cloned.1.call-update
  15.0 0.0 all-gather.5.cloned.1.call-start
  15.1 0.7 all-gather.5.cloned.1.call-update
  15.8 96.4 %all-gather.3.cloned.1.call-done = bf16[640,80,128]{2,1,0:T(8,128)(2,1)} async-done(((bf16[40,80,128]{2,1,0:T(8,128)(2,1)}), bf16[640,80,128]{2,1,0:T(8,128)(2,1)}) %all-gather.3.cloned.1.call-update) | async-done | bytes 13107216 | tf_op jit(solution)/shard_map/all_gather | solution.py:35
  112.2 5.6 %all-to-all-start = ((bf16[640,80,128]{2,1,0:T(8,128)(2,1)}), bf16[640,80,128]{2,1,0:T(8,128)(2,1)}, u32[]{:S(2)}, u32[]{:S(2)}) async-start(bf16[640,80,128]{2,1,0:T(8,128)(2,1)} %all-gather.3.cloned.1.call-done), calls=%async_computation | async-start | bytes 26214400 | tf_op jit(solution)/shard_map/all_to_all | solution.py:36
  117.8 1.0 fusion.14
  118.9 265.4 %all-gather.5.cloned.1.call-done = bf16[40,640,128]{2,1,0:T(8,128)(2,1)} async-done(((bf16[40,80,128]{2,1,0:T(8,128)(2,1)}), bf16[40,640,128]{2,1,0:T(8,128)(2,1)}) %all-gather.5.cloned.1.call-update) | async-done | bytes 6553616 | tf_op jit(solution)/shard_map/all_gather | solution.py:38
  384.2 14.0 %copy.16 = bf16[40,8,80,128]{2,0,3,1:T(8,128)(2,1)} copy(bf16[40,8,80,128]{3,2,1,0:T(8,128)(2,1)} %bitcast.22) | data formatting | bytes 13107200 | tf_op jit(solution)/shard_map/reshape | solution.py:40
  398.3 26.6 %copy.15 = bf16[8,80,80,128]{2,1,3,0:T(8,128)(2,1)} copy(bf16[8,80,80,128]{3,2,1,0:T(8,128)(2,1)} %bitcast.2) | data formatting | bytes 26214400 | tf_op jit(solution)/shard_map/all_to_all | solution.py:36
  424.9 19.6 %convert_bitcast_fusion = bf16[8,40,80,128]{2,1,3,0:T(8,128)(2,1)} fusion(bf16[40,8,80,128]{2,0,3,1:T(8,128)(2,1)} %copy.16, bf16[8,80,80,128]{2,1,3,0:T(8,128)(2,1)} %copy.15), kind=kOutput, calls=%fused_computation.4 | convolution fusion | flops 527564800 | bytes 26214400 | tf_op jit(solution)/shard_map/ibkd,jbkd->bijd/dot_general | solution.py:42
  444.5 7.4 %convert_reduce_fusion = (f32[40,80]{1,0:T(8,128)S(1)}, f32[40,80,128]{1,0,2:T(8,128)S(1)}) fusion(bf16[8,40,80,128]{2,1,3,0:T(8,128)(2,1)} %convert_bitcast_fusion), kind=kLoop, calls=%fused_computation | loop fusion | flops 9417600 | bytes 8204800 | tf_op jit(solution)/shard_map/reduce_sum | solution.py:8
  451.9 0.4 multiply_reduce_fusion
  452.3 0.2 copy-done.7
  452.5 0.0 copy-done.8
  452.5 0.5 add_convert_fusion
  453.0 0.3 copy-done.10
  453.3 1.6 multiply_convert_fusion.1
  (24 shorter events, 0.1 us)
Async XLA Ops:
  6.5 4.1 copy-start
  6.5 4.1 copy-start.2
  6.5 4.1 copy-start.4
  6.5 4.1 copy-start.6
  6.5 4.1 copy-start.5
  6.5 105.7 %all-gather.3.cloned.1.call-start = ((), (), s32[]{:S(2)}) async-start(), calls=%async_computation.1 | async-start | bytes 13926400 | tf_op jit(solution)/shard_map/all_gather | solution.py:35
  10.7 1.1 copy-start.9
  15.0 369.2 %all-gather.5.cloned.1.call-start = ((), (), s32[]{:S(2)}) async-start(), calls=%async_computation.2 | async-start | bytes 7372800 | tf_op jit(solution)/shard_map/all_gather | solution.py:38
  15.8 102.0 %copy-start.3 = (bf16[128,128]{1,0:T(8,128)(2,1)S(1)}, bf16[128,128]{1,0:T(8,128)(2,1)}, u32[]{:S(2)}) copy-start(bf16[128,128]{1,0:T(8,128)(2,1)} %param.19) | copy-start | bytes 98308
  112.2 286.1 %all-to-all-start = ((bf16[640,80,128]{2,1,0:T(8,128)(2,1)}), bf16[640,80,128]{2,1,0:T(8,128)(2,1)}, u32[]{:S(2)}, u32[]{:S(2)}) async-start(bf16[640,80,128]{2,1,0:T(8,128)(2,1)} %all-gather.3.cloned.1.call-done), calls=%async_computation | async-start | bytes 26214400 | tf_op jit(solution)/shard_map/all_to_all | solution.py:36
  451.9 0.7 copy-start.7
  451.9 0.7 copy-start.8
  452.5 0.8 copy-start.10
  453.3 1.6 copy-start.1
Sparse Core Ops, SparseCore 0:
  15.1 97.0 all-gather.2
  113.8 270.3 all-gather.4
where the time goes:
time: 464 us; the launch traced here: 462 us
  waiting for transfers between devices  363 us (78%)
  local copies, waits for them, and re-layouts  42.7 us (9%)
  matrix products  25 us (5%)
  between operations  13.6 us (3%)
  other arithmetic  12.3 us (3%)
  starting transfers between devices  5.67 us (1%)
    all_gather x1, waiting for transfers between devices, body(): piece = lax.all_gather(left, 'col', axis=1, tiled=True)  265 us
    all_gather x1, waiting for transfers between devices, body(): right_all = lax.all_gather(right, 'row', axis=0, tiled=True)  96.4 us
    all_to_all x1, local copies, waits for them, and re-layouts, body(): lax.all_to_all(right_all, 'col', split_axis=0, concat_axis=1, tiled=True)  26.6 us
    dot_general x1, matrix products, body(): jnp.einsum('ibkd,jbkd->bijd', left_parts, right_parts, preferred_element_...  19.6 us
    reshape x1, local copies, waits for them, and re-layouts, body(): left_parts = piece.reshape(piece.shape[0], count, width, hidden)  14 us
  transfers between devices with their start and end apart: 3, of which 2 were waited for; matrix products, arithmetic and copies ran while one was open for 3% of the time, Pallas kernels for 0%

commit v1 on v0

v1 whole, which is shorter than its diff:
```python
import functools

import jax
import jax.numpy as jnp
from jax import lax
from jax.experimental import pallas as pl
from jax.experimental.pallas import tpu as pltpu
from jax.sharding import PartitionSpec as P

MESH = pl.DeviceIdType.MESH
F32, BF16 = jnp.float32, jnp.bfloat16
NT = (((1,), (1,)), ((), ()))
CHIPS = 64
ROWS = 112
BACK = 32


def device(x, y, z, core):
    return (y * 4 + (z // 2) * 2 + core, x * 2 + z % 2)


def chip_index(x, y, z):
    return (y * 2 + z // 2) * 8 + x * 2 + z % 2


def kernel(
    pair, mask, norm_gain, norm_bias, proj_w, gate_w, out_gain, out_bias, out_w, out_gate_w,
    out,
    normed, masked, gating, weights, wide, packed, arrived, left, right, swap, combined, back, returned, finished,
    sibling_send, sibling_recv, send, recv, back_send, back_recv, local,
):
    r, c = lax.axis_index("row"), lax.axis_index("col")
    x, y, z, core = c // 2, r // 4, ((r // 2) % 2) * 2 + c % 2, r % 2
    me = chip_index(x, y, z)

    def shifted(step):
        return (x + step // 16) % 4, (y + (step // 4) % 4) % 4, (z + step % 4) % 4

    barrier = pltpu.get_barrier_semaphore()

    def greet(step, carry):
        pl.semaphore_signal(
            barrier, inc=1, device_id=device(*shifted(step // 2), (core + step % 2) % 2), device_id_type=MESH
        )
        return carry

    lax.fori_loop(1, 2 * CHIPS, greet, 0)

    swap[0:128, 0:128] = jnp.zeros((128, 128), BF16)
    swap[0:40, 0:80] = mask[...].astype(F32).astype(BF16)
    mask_t = jnp.transpose(swap[0:128, 0:128].astype(F32))[0:80, :].astype(BF16)
    gain, bias = norm_gain[...], norm_bias[...]

    def norm_row(i, carry):
        values = pair[i].astype(F32)
        mean = jnp.mean(values, axis=-1, keepdims=True)
        centred = values - mean
        var = jnp.mean(centred * centred, axis=-1, keepdims=True)
        n = (centred * lax.rsqrt(var + 1e-05) * gain + bias).astype(BF16)
        normed[i] = n
        pick = (lax.broadcasted_iota(jnp.int32, (128, 128), 0) == i).astype(F32).astype(BF16)
        valid = jnp.dot(mask_t, pick, preferred_element_type=F32)
        masked[core, i] = (n.astype(F32) * valid).astype(BF16)
        return carry

    lax.fori_loop(0, 40, norm_row, 0)
    pl.semaphore_wait(barrier, 2 * CHIPS - 1)

    to_sibling = pltpu.make_async_remote_copy(
        src_ref=masked.at[core],
        dst_ref=masked.at[core],
        send_sem=sibling_send,
        recv_sem=sibling_recv,
        device_id=(r + 1 - 2 * core, c),
        device_id_type=MESH,
    )
    to_sibling.start()

    half = pl.ds(pl.multiple_of(core * 64, 64), 64)
    for n, w in enumerate((proj_w, gate_w)):
        for side in range(2):
            turned = jnp.transpose(w[:, side * 128 : side * 128 + 128].astype(F32))
            finished[0:128, :] = turned
            weights[n * 128 + side * 64 : n * 128 + side * 64 + 64, :] = finished[half, :].astype(BF16)
    to_sibling.wait()

    lane = lax.broadcasted_iota(jnp.int32, (64, 128), 1)

    def project(row, carry):
        who, inner = row // 8, row % 8

        def block(p):
            return masked[who, (p // 5) * 8 + inner, (p % 5) * 16 : (p % 5) * 16 + 16, :]

        tokens = [block(p) for p in range(24)] + [block(24), block(24), jnp.zeros((96, 128), BF16)]
        both = lax.dot_general(weights[...], jnp.concatenate(tokens, axis=0), NT, preferred_element_type=F32)
        value = both[:128] * jax.nn.sigmoid(both[128:])
        for g in range(3):
            wide[pl.ds(g * 16 + row, 64, stride=ROWS), :] = value[:64, g * 128 : g * 128 + 128]
            wide[pl.ds(48 + g * 16 + row, 64, stride=ROWS), :] = value[64:, g * 128 : g * 128 + 128]
        wide[pl.ds(96 + row, 64, stride=ROWS), :] = jnp.where(lane < 16, value[:64, 384:], value[64:, 384:])
        return carry

    lax.fori_loop(0, 16, project, 0)

    def narrow(m, carry):
        packed[m] = wide[pl.ds(pl.multiple_of(m * ROWS, ROWS), ROWS), :].astype(BF16)
        return carry

    lax.fori_loop(0, CHIPS, narrow, 0)

    keep = pltpu.make_async_copy(packed.at[me], arrived.at[me], local)
    keep.start()

    def post(step, carry):
        there = shifted(step)
        pltpu.make_async_remote_copy(
            src_ref=packed.at[chip_index(*there)],
            dst_ref=arrived.at[me],
            send_sem=send,
            recv_sem=recv,
            device_id=device(*there, core),
            device_id_type=MESH,
        ).start()
        return carry

    lax.fori_loop(1, CHIPS, post, 0)

    def gate_row(i, carry):
        gating[i] = jax.nn.sigmoid(jnp.dot(normed[i], out_gate_w[...], preferred_element_type=F32))
        return carry

    lax.fori_loop(0, 40, gate_row, 0)
    for a in range(8):
        at = lax.broadcasted_iota(jnp.int32, (128, 1024), 0)
        to = lax.broadcasted_iota(jnp.int32, (128, 1024), 1)
        swap[a * 128 : a * 128 + 128, :] = (to == (at // 16) * 128 + a * 16 + at % 16).astype(F32).astype(BF16)
    w_t = jnp.transpose(out_w[...].astype(F32))
    shift = lax.dot_general(out_bias[...], w_t, NT, preferred_element_type=F32, precision=lax.Precision.HIGHEST)
    scaled = jnp.transpose(w_t * out_gain[...]).astype(BF16)

    keep.wait()
    whole = pltpu.make_async_remote_copy(
        src_ref=packed.at[pl.ds(0, CHIPS - 1)],
        dst_ref=arrived.at[pl.ds(0, CHIPS - 1)],
        send_sem=send,
        recv_sem=recv,
        device_id=(r + 1 - 2 * core, c),
        device_id_type=MESH,
    )
    whole.wait_recv()

    for g in range(7):
        beside = [
            jnp.concatenate([arrived[m * 8 + k, g * 16 : g * 16 + 16, :] for m in range(8)], axis=0)
            for k in range(8)
        ]
        lanes = 1024 if g < 6 else 256
        moved = jnp.dot(jnp.concatenate(beside, axis=1), swap[:, :lanes], preferred_element_type=F32).astype(BF16)
        for s in range(8 if g < 6 else 2):
            p = (g % 3) * 8 + s if g < 6 else 24
            target = left if (g < 3 or (g == 6 and s == 0)) else right
            target[(p // 5) * 128 : (p // 5) * 128 + 128, (p % 5) * 128 : (p % 5) * 128 + 128] = (
                moved[:, s * 128 : s * 128 + 128]
            )

    for n in range(5):
        rows = pl.ds(n * 128, 128)
        combined[rows, :] = lax.dot_general(left[rows, :], right[...], NT, preferred_element_type=F32).astype(BF16)

    for pair_of in range(2):
        moved = []
        for g in (2 * pair_of, 2 * pair_of + 1):
            blocks = [p for p in range(8 * g, 8 * g + 8) if p < 25]
            beside = [
                combined[(p // 5) * 128 : (p // 5) * 128 + 128, (p % 5) * 128 : (p % 5) * 128 + 128] for p in blocks
            ]
            moved.append(
                jnp.dot(
                    jnp.concatenate(beside, axis=1), swap[: 128 * len(blocks), :], preferred_element_type=F32
                )
            )
        for m in range(8):
            for k in range(8):
                for h in range(2):
                    tile = [v[m * 16 + h * 8 : m * 16 + h * 8 + 8, k * 128 : k * 128 + 128] for v in moved]
                    back[(m * 8 + k) * 2 + h, pair_of * 16 : pair_of * 16 + 16, :] = jnp.concatenate(
                        tile, axis=0
                    ).astype(BF16)

    mine = core * CHIPS + me
    keep_back = pltpu.make_async_copy(back.at[me * 2 + core], returned.at[mine], local)
    keep_back.start()

    def post_back(step, carry):
        there, to_core = shifted(step // 2), (core + step % 2) % 2
        pltpu.make_async_remote_copy(
            src_ref=back.at[chip_index(*there) * 2 + to_core],
            dst_ref=returned.at[mine],
            send_sem=back_send,
            recv_sem=back_recv,
            device_id=device(*there, to_core),
            device_id_type=MESH,
        ).start()
        return carry

    lax.fori_loop(1, 2 * CHIPS, post_back, 0)
    keep_back.wait()
    whole_back = pltpu.make_async_remote_copy(
        src_ref=back.at[pl.ds(0, 2 * CHIPS - 1)],
        dst_ref=returned.at[pl.ds(0, 2 * CHIPS - 1)],
        send_sem=back_send,
        recv_sem=back_recv,
        device_id=(r + 1 - 2 * core, c),
        device_id_type=MESH,
    )
    whole_back.wait_recv()

    def total(ch, carry):
        return carry + returned[ch].astype(F32)

    mean = lax.fori_loop(0, 128, total, jnp.zeros((BACK, 128), F32), unroll=8) * (1 / 128)

    def spread(ch, carry):
        centred = returned[ch].astype(F32) - mean
        return carry + centred * centred

    var = lax.fori_loop(0, 128, spread, jnp.zeros((BACK, 128), F32), unroll=8) * (1 / 128)
    scale = lax.rsqrt(var + 1e-05)

    def normalise(ch, carry):
        finished[pl.ds(pl.multiple_of(ch * BACK, BACK), BACK), :] = (returned[ch].astype(F32) - mean) * scale
        return carry

    lax.fori_loop(0, 128, normalise, 0, unroll=8)

    def finish(inner, carry):
        for g in range(4):
            blocks = [p for p in range(8 * g, 8 * g + 8) if p < 25]
            values = finished[pl.ds(g * 8 + inner, 128, stride=BACK), :]
            tokens = jnp.transpose(values)[: 16 * len(blocks), :].astype(BF16)
            projected = jnp.dot(tokens, scaled, preferred_element_type=F32) + shift
            for s, p in enumerate(blocks):
                at = (p // 5) * 8 + inner
                for h in range(2):
                    cols = pl.ds(h * 40 + (p % 5) * 8, 8)
                    rows = projected[s * 16 + h * 8 : s * 16 + h * 8 + 8, :]
                    out[at, cols, :] = (rows * gating[at, cols, :]).astype(BF16)
        return carry

    lax.fori_loop(0, 8, finish, 0)
    whole.wait_send()
    whole_back.wait_send()


def body(*args):
    pair, mask, norm_gain, norm_bias, proj_w, gate_w, out_gain, out_bias, out_w, out_gate_w = args
    dma = pltpu.SemaphoreType.DMA
    return pl.pallas_call(
        kernel,
        out_shape=jax.ShapeDtypeStruct(pair.shape, BF16),
        in_specs=[pl.BlockSpec(memory_space=pltpu.VMEM)] * 10,
        out_specs=pl.BlockSpec(memory_space=pltpu.VMEM),
        scratch_shapes=[
            pltpu.VMEM((40, 80, 128), BF16),
            pltpu.VMEM((2, 40, 80, 128), BF16),
            pltpu.VMEM((40, 80, 128), F32),
            pltpu.VMEM((256, 128), BF16),
            pltpu.VMEM((CHIPS * ROWS, 128), F32),
            pltpu.VMEM((CHIPS, ROWS, 128), BF16),
            pltpu.VMEM((CHIPS, ROWS, 128), BF16),
            pltpu.VMEM((640, 640), BF16),
            pltpu.VMEM((640, 640), BF16),
            pltpu.VMEM((1024, 1024), BF16),
            pltpu.VMEM((640, 640), BF16),
            pltpu.VMEM((2 * CHIPS, BACK, 128), BF16),
            pltpu.VMEM((2 * CHIPS, BACK, 128), BF16),
            pltpu.VMEM((128 * BACK, 128), F32),
            dma, dma, dma, dma, dma, dma, dma,
        ],
        compiler_params=pltpu.CompilerParams(
            collective_id=0, has_side_effects=True, vmem_limit_bytes=56 * 2**20
        ),
    )(
        pair, mask, norm_gain.reshape(1, 128), norm_bias.reshape(1, 128), proj_w, gate_w,
        out_gain.reshape(1, 128), out_bias.reshape(1, 128), out_w, out_gate_w,
    )


def solution(mesh):
    placed = (P("row", "col", None), P("row", "col"), P(), P(), P(), P(), P(), P(), P(), P())
    return jax.shard_map(body, mesh=mesh, in_specs=placed, out_specs=P("row", "col", None), check_vma=False)
```

time: 464 us -> 88.2 us (0.19)
  waiting for transfers between devices: 363 us -> 0 us
  Pallas kernels: 0 us -> 85.9 us
  local copies, waits for them, and re-layouts: 42.7 us -> 2.09 us
  matrix products: 25 us -> 0 us
  between operations: 13.6 us -> 0.01 us
  other arithmetic: 12.3 us -> 0 us
  starting transfers between devices: 5.67 us -> 0 us
    all_gather x2 -> x0, waiting for transfers between devices: 362 us -> none  [the longest x1 265 us: body(): piece = lax.all_gather(left, 'col', axis=1, tiled=True)]
    pallas_call x0 -> x1, Pallas kernels: none -> 85.9 us  [body(): pl.pallas_call(kernel, out_shape=jax.ShapeDtypeStruct(pair.shape, BF16),...]
    all_to_all x1 -> x0, local copies, waits for them, and re-layouts: 26.6 us -> none  [body(): lax.all_to_all(right_all, 'col', split_axis=0, concat_axis=1, tiled=True)]
    dot_general x5 -> x0, matrix products: 25 us -> none  [the longest x1 19.6 us: body(): jnp.einsum('ibkd,jbkd->bijd', left_parts, right_parts, preferred_element_...]
    reshape x1 -> x0, local copies, waits for them, and re-layouts: 14 us -> none  [body(): left_parts = piece.reshape(piece.shape[0], count, width, hidden)]
    reduce_sum x4 -> x0, other arithmetic: 11.8 us -> none  [the longest x2 9.03 us: layer_norm(): mean = jnp.mean(values, axis=-1, keepdims=True)]
    all_to_all x1 -> x0, starting transfers between devices: 5.59 us -> none  [body(): lax.all_to_all(right_all, 'col', split_axis=0, concat_axis=1, tiled=True)]
  transfers between devices with their start and end apart: 3 -> 0, of which waited for: 2 -> 0; matrix products, arithmetic and copies ran while one was open for 3% -> 0% of each run, Pallas kernels for 0% -> 0%
where the time goes in v1:
time: 88.2 us; the launch traced here: 88 us
  Pallas kernels  85.9 us (97%)
  local copies, waits for them, and re-layouts  2.09 us (2%)
    pallas_call x1, Pallas kernels, body(): pl.pallas_call(kernel, out_shape=jax.ShapeDtypeStruct(pair.shape, BF16),...  85.9 us
    unnamed x1, local copies, waits for them, and re-layouts  2.09 us

profile of v1, /device:TPU:1, one launch (start us, length us, event | category | flops | bytes accessed | tf_op | source)
XLA Modules:
  0.0 88.0 jit_solution(6712402381092949350)
XLA Ops:
  0.0 85.9 %shard_map.100 = bf16[40,80,128]{2,1,0:T(8,128)(2,1)} custom-call(bf16[40,80,128]{2,1,0:T(8,128)(2,1)} %pair.1, s32[40,80]{1,0:T(8,128)} %mask.1, f32[1,128]{1,0:T(1,128)} %bitcast.4, f32[1,128]{1,0:T(1,128)} %bitcast.5, bf16[128,256]{1,0:T(8,128)(2,1)} %proj_w.1, bf16[128,256]{1,0:T(8,128)(2,1)} %gate_w.1, f32[1,128]{1,0:T(1,128)} %bitcast.6, ...), custom_call_target="tpu_custom_call" | custom-call | tf_op jit(solution)/shard_map/pallas_call | solution.py:259
  85.9 2.1 %copy.12 = bf16[40,80,128]{2,1,0:T(8,128)(2,1)} copy(bf16[40,80,128]{2,1,0:T(8,128)(2,1)} %shard_map.100) | data formatting | bytes 1638400

commit v2 on v1

--- a/solution.py
+++ b/solution.py
@@ -23,28 +23,37 @@
     return (y * 2 + z // 2) * 8 + x * 2 + z % 2
 
 
+def distance(shift):
+    return sum(min(d, 4 - d) for d in shift)
+
+
+SHIFTS = sorted(
+    [(n // 16, n // 4 % 4, n % 4) for n in range(1, CHIPS)], key=lambda s: (-distance(s), (s[0] * 7 + s[1] * 11 + s[2] * 13) % 16)
+)
+
+
 def kernel(
     pair, mask, norm_gain, norm_bias, proj_w, gate_w, out_gain, out_bias, out_w, out_gate_w,
     out,
     normed, masked, gating, weights, wide, packed, arrived, left, right, swap, combined, back, returned, finished,
-    sibling_send, sibling_recv, send, recv, back_send, back_recv, local,
+    sibling_send, sibling_recv, send, recv, back_send, back_recv, local, entered_y, entered_z,
 ):
     r, c = lax.axis_index("row"), lax.axis_index("col")
     x, y, z, core = c // 2, r // 4, ((r // 2) % 2) * 2 + c % 2, r % 2
     me = chip_index(x, y, z)
 
-    def shifted(step):
-        return (x + step // 16) % 4, (y + (step // 4) % 4) % 4, (z + step % 4) % 4
+    def shifted(dx, dy, dz):
+        return (x + dx) % 4, (y + dy) % 4, (z + dz) % 4
 
     barrier = pltpu.get_barrier_semaphore()
-
-    def greet(step, carry):
-        pl.semaphore_signal(
-            barrier, inc=1, device_id=device(*shifted(step // 2), (core + step % 2) % 2), device_id_type=MESH
-        )
-        return carry
-
-    lax.fori_loop(1, 2 * CHIPS, greet, 0)
+    sibling = device(x, y, z, 1 - core)
+    along = [[device(*shifted(*(d * (a == n) for a in range(3))), core) for d in (1, 2, 3)] for n in range(3)]
+    for there in [sibling] + along[0] + along[1] + along[2]:
+        pl.semaphore_signal(barrier, inc=1, device_id=there, device_id_type=MESH)
+
+    def pass_on(sem, line):
+        for there in line:
+            pl.semaphore_signal(sem, inc=1, device_id=there, device_id_type=MESH)
 
     swap[0:128, 0:128] = jnp.zeros((128, 128), BF16)
     swap[0:40, 0:80] = mask[...].astype(F32).astype(BF16)
@@ -63,15 +72,21 @@
         masked[core, i] = (n.astype(F32) * valid).astype(BF16)
         return carry
 
-    lax.fori_loop(0, 40, norm_row, 0)
-    pl.semaphore_wait(barrier, 2 * CHIPS - 1)
+    lax.fori_loop(0, 16, norm_row, 0)
+    pl.semaphore_wait(barrier, 10)
+    pass_on(entered_y, along[1])
+    lax.fori_loop(16, 28, norm_row, 0)
+    pl.semaphore_wait(entered_y, 3)
+    pass_on(entered_z, along[2])
+    lax.fori_loop(28, 40, norm_row, 0)
+    pl.semaphore_wait(entered_z, 3)
 
     to_sibling = pltpu.make_async_remote_copy(
         src_ref=masked.at[core],
         dst_ref=masked.at[core],
         send_sem=sibling_send,
         recv_sem=sibling_recv,
-        device_id=(r + 1 - 2 * core, c),
+        device_id=sibling,
         device_id_type=MESH,
     )
     to_sibling.start()
@@ -112,8 +127,8 @@
     keep = pltpu.make_async_copy(packed.at[me], arrived.at[me], local)
     keep.start()
 
-    def post(step, carry):
-        there = shifted(step)
+    for shift in SHIFTS:
+        there = shifted(*shift)
         pltpu.make_async_remote_copy(
             src_ref=packed.at[chip_index(*there)],
             dst_ref=arrived.at[me],
@@ -122,9 +137,6 @@
             device_id=device(*there, core),
             device_id_type=MESH,
         ).start()
-        return carry
-
-    lax.fori_loop(1, CHIPS, post, 0)
 
     def gate_row(i, carry):
         gating[i] = jax.nn.sigmoid(jnp.dot(normed[i], out_gate_w[...], preferred_element_type=F32))
@@ -136,7 +148,7 @@
         to = lax.broadcasted_iota(jnp.int32, (128, 1024), 1)
         swap[a * 128 : a * 128 + 128, :] = (to == (at // 16) * 128 + a * 16 + at % 16).astype(F32).astype(BF16)
     w_t = jnp.transpose(out_w[...].astype(F32))
-    shift = lax.dot_general(out_bias[...], w_t, NT, preferred_element_type=F32, precision=lax.Precision.HIGHEST)
+    offset = lax.dot_general(out_bias[...], w_t, NT, preferred_element_type=F32, precision=lax.Precision.HIGHEST)
     scaled = jnp.transpose(w_t * out_gain[...]).astype(BF16)
 
     keep.wait()
@@ -145,7 +157,7 @@
         dst_ref=arrived.at[pl.ds(0, CHIPS - 1)],
         send_sem=send,
         recv_sem=recv,
-        device_id=(r + 1 - 2 * core, c),
+        device_id=sibling,
         device_id_type=MESH,
     )
     whole.wait_recv()
@@ -192,8 +204,8 @@
     keep_back = pltpu.make_async_copy(back.at[me * 2 + core], returned.at[mine], local)
     keep_back.start()
 
-    def post_back(step, carry):
-        there, to_core = shifted(step // 2), (core + step % 2) % 2
+    for shift, other in [(s, o) for s in SHIFTS for o in (0, 1)] + [((0, 0, 0), 1)]:
+        there, to_core = shifted(*shift), (core + other) % 2
         pltpu.make_async_remote_copy(
             src_ref=back.at[chip_index(*there) * 2 + to_core],
             dst_ref=returned.at[mine],
@@ -202,16 +214,13 @@
             device_id=device(*there, to_core),
             device_id_type=MESH,
         ).start()
-        return carry
-
-    lax.fori_loop(1, 2 * CHIPS, post_back, 0)
     keep_back.wait()
     whole_back = pltpu.make_async_remote_copy(
         src_ref=back.at[pl.ds(0, 2 * CHIPS - 1)],
         dst_ref=returned.at[pl.ds(0, 2 * CHIPS - 1)],
         send_sem=back_send,
         recv_sem=back_recv,
-        device_id=(r + 1 - 2 * core, c),
+        device_id=sibling,
         device_id_type=MESH,
     )
     whole_back.wait_recv()
@@ -239,7 +248,7 @@
             blocks = [p for p in range(8 * g, 8 * g + 8) if p < 25]
             values = finished[pl.ds(g * 8 + inner, 128, stride=BACK), :]
             tokens = jnp.transpose(values)[: 16 * len(blocks), :].astype(BF16)
-            projected = jnp.dot(tokens, scaled, preferred_element_type=F32) + shift
+            projected = jnp.dot(tokens, scaled, preferred_element_type=F32) + offset
             for s, p in enumerate(blocks):
                 at = (p // 5) * 8 + inner
                 for h in range(2):
@@ -276,7 +285,7 @@
             pltpu.VMEM((2 * CHIPS, BACK, 128), BF16),
             pltpu.VMEM((2 * CHIPS, BACK, 128), BF16),
             pltpu.VMEM((128 * BACK, 128), F32),
-            dma, dma, dma, dma, dma, dma, dma,
+            dma, dma, dma, dma, dma, dma, dma, pltpu.SemaphoreType.REGULAR, pltpu.SemaphoreType.REGULAR,
         ],
         compiler_params=pltpu.CompilerParams(
             collective_id=0, has_side_effects=True, vmem_limit_bytes=56 * 2**20

time: 88.2 us -> 70.9 us (0.80)
  Pallas kernels: 85.9 us -> 68.6 us
    pallas_call x1, Pallas kernels: 85.9 us -> 68.6 us  [body(): pl.pallas_call(kernel, out_shape=jax.ShapeDtypeStruct(pair.shape, BF16),...]
where the time goes in v2:
time: 70.9 us; the launch traced here: 70.7 us
  Pallas kernels  68.6 us (97%)
  local copies, waits for them, and re-layouts  2.09 us (3%)
    pallas_call x1, Pallas kernels, body(): pl.pallas_call(kernel, out_shape=jax.ShapeDtypeStruct(pair.shape, BF16),...  68.6 us
    unnamed x1, local copies, waits for them, and re-layouts  2.09 us

profile of v2, /device:TPU:1, one launch (start us, length us, event | category | flops | bytes accessed | tf_op | source)
XLA Modules:
  0.0 70.7 jit_solution(16434733410778581546)
XLA Ops:
  0.0 68.6 %shard_map.100 = bf16[40,80,128]{2,1,0:T(8,128)(2,1)} custom-call(bf16[40,80,128]{2,1,0:T(8,128)(2,1)} %pair.1, s32[40,80]{1,0:T(8,128)} %mask.1, f32[1,128]{1,0:T(1,128)} %bitcast.4, f32[1,128]{1,0:T(1,128)} %bitcast.5, bf16[128,256]{1,0:T(8,128)(2,1)} %proj_w.1, bf16[128,256]{1,0:T(8,128)(2,1)} %gate_w.1, f32[1,128]{1,0:T(1,128)} %bitcast.6, ...), custom_call_target="tpu_custom_call" | custom-call | tf_op jit(solution)/shard_map/pallas_call | solution.py:268
  68.6 2.1 %copy.12 = bf16[40,80,128]{2,1,0:T(8,128)(2,1)} copy(bf16[40,80,128]{2,1,0:T(8,128)(2,1)} %shard_map.100) | data formatting | bytes 1638400

commit v3 on v2

--- a/solution.py
+++ b/solution.py
@@ -11,7 +11,7 @@
 F32, BF16 = jnp.float32, jnp.bfloat16
 NT = (((1,), (1,)), ((), ()))
 CHIPS = 64
-ROWS = 112
+ROWS = 104
 BACK = 32
 
 
@@ -21,6 +21,10 @@
 
 def chip_index(x, y, z):
     return (y * 2 + z // 2) * 8 + x * 2 + z % 2
+
+
+def channel_of(x, y, z):
+    return x * 16 + y * 4 + z
 
 
 def distance(shift):
@@ -35,12 +39,12 @@
 def kernel(
     pair, mask, norm_gain, norm_bias, proj_w, gate_w, out_gain, out_bias, out_w, out_gate_w,
     out,
-    normed, masked, gating, weights, wide, packed, arrived, left, right, swap, combined, back, returned, finished,
+    normed, masks, gating, weights, wide, packed, arrived, left, right, swap, combined, back, returned, finished,
     sibling_send, sibling_recv, send, recv, back_send, back_recv, local, entered_y, entered_z,
 ):
     r, c = lax.axis_index("row"), lax.axis_index("col")
     x, y, z, core = c // 2, r // 4, ((r // 2) % 2) * 2 + c % 2, r % 2
-    me = chip_index(x, y, z)
+    me, channel = chip_index(x, y, z), channel_of(x, y, z)
 
     def shifted(dx, dy, dz):
         return (x + dx) % 4, (y + dy) % 4, (z + dz) % 4
@@ -55,91 +59,131 @@
         for there in line:
             pl.semaphore_signal(sem, inc=1, device_id=there, device_id_type=MESH)
 
-    swap[0:128, 0:128] = jnp.zeros((128, 128), BF16)
-    swap[0:40, 0:80] = mask[...].astype(F32).astype(BF16)
-    mask_t = jnp.transpose(swap[0:128, 0:128].astype(F32))[0:80, :].astype(BF16)
+    lane = lax.broadcasted_iota(jnp.int32, (8, 128), 1)
+    finished[0:40, 0:128] = jnp.zeros((40, 128), F32)
+    finished[0:40, 0:80] = mask[...].astype(F32)
+    for g in range(3):
+        valid = jnp.zeros((8, 128), F32)
+        for s in range(8):
+            p = 8 * g + s
+            turned = pltpu.roll(finished[p // 5 * 8 : p // 5 * 8 + 8, :], (s - p % 5) * 16 % 128, 1)
+            valid = jnp.where(lane // 16 == s, turned, valid)
+        masks[core, g * 8 : g * 8 + 8, :] = valid
+    last = jnp.zeros((8, 128), F32)
+    for n in range(8):
+        turned = pltpu.roll(jnp.broadcast_to(finished[32 + n : 33 + n, :], (8, 128)), (n - 4) * 16 % 128, 1)
+        last = jnp.where(lane // 16 == n, turned, last)
+    masks[core, 24:32, :] = last
+
     gain, bias = norm_gain[...], norm_bias[...]
 
-    def norm_row(i, carry):
-        values = pair[i].astype(F32)
+    def norm_rows(n, carry):
+        values = pair[pl.ds(n * 4, 4)].astype(F32)
         mean = jnp.mean(values, axis=-1, keepdims=True)
         centred = values - mean
         var = jnp.mean(centred * centred, axis=-1, keepdims=True)
-        n = (centred * lax.rsqrt(var + 1e-05) * gain + bias).astype(BF16)
-        normed[i] = n
-        pick = (lax.broadcasted_iota(jnp.int32, (128, 128), 0) == i).astype(F32).astype(BF16)
-        valid = jnp.dot(mask_t, pick, preferred_element_type=F32)
-        masked[core, i] = (n.astype(F32) * valid).astype(BF16)
+        normed[core, pl.ds(n * 4, 4)] = (centred * lax.rsqrt(var + 1e-05) * gain + bias).astype(BF16)
         return carry
 
-    lax.fori_loop(0, 16, norm_row, 0)
+    def to_sibling(ref, send_sem, recv_sem):
+        return pltpu.make_async_remote_copy(
+            src_ref=ref, dst_ref=ref, send_sem=send_sem, recv_sem=recv_sem, device_id=sibling, device_id_type=MESH
+        )
+
+    exchange = [
+        to_sibling(masks.at[core], sibling_send.at[0], sibling_recv.at[0]),
+        to_sibling(normed.at[core, pl.ds(0, 20)], sibling_send.at[1], sibling_recv.at[1]),
+        to_sibling(normed.at[core, pl.ds(20, 20)], sibling_send.at[2], sibling_recv.at[2]),
+    ]
+    lax.fori_loop(0, 5, norm_rows, 0)
     pl.semaphore_wait(barrier, 10)
+    exchange[0].start()
+    exchange[1].start()
     pass_on(entered_y, along[1])
-    lax.fori_loop(16, 28, norm_row, 0)
-    pl.semaphore_wait(entered_y, 3)
-    pass_on(entered_z, along[2])
-    lax.fori_loop(28, 40, norm_row, 0)
-    pl.semaphore_wait(entered_z, 3)
-
-    to_sibling = pltpu.make_async_remote_copy(
-        src_ref=masked.at[core],
-        dst_ref=masked.at[core],
-        send_sem=sibling_send,
-        recv_sem=sibling_recv,
-        device_id=sibling,
-        device_id_type=MESH,
-    )
-    to_sibling.start()
+    lax.fori_loop(5, 10, norm_rows, 0)
+    exchange[2].start()
 
     half = pl.ds(pl.multiple_of(core * 64, 64), 64)
     for n, w in enumerate((proj_w, gate_w)):
         for side in range(2):
-            turned = jnp.transpose(w[:, side * 128 : side * 128 + 128].astype(F32))
-            finished[0:128, :] = turned
-            weights[n * 128 + side * 64 : n * 128 + side * 64 + 64, :] = finished[half, :].astype(BF16)
-    to_sibling.wait()
-
-    lane = lax.broadcasted_iota(jnp.int32, (64, 128), 1)
-
-    def project(row, carry):
-        who, inner = row // 8, row % 8
-
-        def block(p):
-            return masked[who, (p // 5) * 8 + inner, (p % 5) * 16 : (p % 5) * 16 + 16, :]
-
-        tokens = [block(p) for p in range(24)] + [block(24), block(24), jnp.zeros((96, 128), BF16)]
-        both = lax.dot_general(weights[...], jnp.concatenate(tokens, axis=0), NT, preferred_element_type=F32)
-        value = both[:128] * jax.nn.sigmoid(both[128:])
-        for g in range(3):
-            wide[pl.ds(g * 16 + row, 64, stride=ROWS), :] = value[:64, g * 128 : g * 128 + 128]
-            wide[pl.ds(48 + g * 16 + row, 64, stride=ROWS), :] = value[64:, g * 128 : g * 128 + 128]
-        wide[pl.ds(96 + row, 64, stride=ROWS), :] = jnp.where(lane < 16, value[:64, 384:], value[64:, 384:])
-        return carry
-
-    lax.fori_loop(0, 16, project, 0)
-
-    def narrow(m, carry):
-        packed[m] = wide[pl.ds(pl.multiple_of(m * ROWS, ROWS), ROWS), :].astype(BF16)
-        return carry
-
-    lax.fori_loop(0, CHIPS, narrow, 0)
-
-    keep = pltpu.make_async_copy(packed.at[me], arrived.at[me], local)
+            finished[0:128, :] = jnp.transpose(w[:, side * 128 : side * 128 + 128].astype(F32))
+            mine = finished[half, :].astype(BF16)
+            for a in range(4):
+                weights[a, (n * 2 + side) * 16 : (n * 2 + side) * 16 + 16, :] = mine[a * 16 : a * 16 + 16, :]
+
+    def project(who, xs):
+        both_x = jnp.concatenate([weights[a] for a in xs], axis=0)
+
+        def values_of(tokens, valid):
+            got = lax.dot_general(both_x, tokens, NT, preferred_element_type=F32)
+            proj = jnp.concatenate([got[0:32], got[64:96]], axis=0)
+            gate = jnp.concatenate([got[32:64], got[96:128]], axis=0)
+            return proj * (0.5 * jnp.tanh(0.5 * gate) + 0.5) * valid
+
+        def put(values, row, side_rows):
+            for n, a in enumerate(xs):
+                for side in range(2):
+                    wide[pl.ds(a * (16 * ROWS) + side * side_rows + row, 16, stride=ROWS), :] = values[
+                        (2 * n + side) * 16 : (2 * n + side) * 16 + 16
+                    ]
+
+        def project_row(inner, carry):
+            tokens = [
+                normed[who, (p // 5) * 8 + inner, (p % 5) * 16 : (p % 5) * 16 + 16, :] for p in range(24)
+            ]
+            valid = jnp.concatenate([masks[who, pl.ds(g * 8 + inner, 1), :] for g in range(3)], axis=1)
+            values = values_of(jnp.concatenate(tokens, axis=0), valid)
+            for g in range(3):
+                put(values[:, g * 128 : g * 128 + 128], g * 16 + who * 8 + inner, 48)
+            return carry
+
+        lax.fori_loop(0, 8, project_row, 0)
+        last_tokens = [normed[who, 32 + n, 64:80, :] for n in range(8)]
+        put(values_of(jnp.concatenate(last_tokens, axis=0), masks[who, 24:25, :]), 96 + who, 2)
+
+    def narrow(a):
+        def one(n, carry):
+            m = a * 16 + n
+            packed[m] = wide[pl.ds(pl.multiple_of(m * ROWS, 8), ROWS), :].astype(BF16)
+            return carry
+
+        lax.fori_loop(0, 16, one, 0, unroll=4)
+
+    def post(dxs):
+        for shift in SHIFTS:
+            if shift[0] in dxs:
+                there = shifted(*shift)
+                pltpu.make_async_remote_copy(
+                    src_ref=packed.at[channel_of(*there)],
+                    dst_ref=arrived.at[me],
+                    send_sem=send,
+                    recv_sem=recv,
+                    device_id=device(*there, core),
+                    device_id_type=MESH,
+                ).start()
+
+    for row in range(100, ROWS):
+        wide[pl.ds(row, CHIPS, stride=ROWS), :] = jnp.zeros((CHIPS, 128), F32)
+    for part, dxs in enumerate(((2, 1), (3, 0))):
+        xs = [(x + dx) % 4 for dx in dxs]
+        project(core, xs)
+        if part == 0:
+            pl.semaphore_wait(entered_y, 3)
+            pass_on(entered_z, along[2])
+            for e in exchange:
+                e.wait()
+        project(1 - core, xs)
+        for a in xs:
+            narrow(a)
+        if part == 0:
+            pl.semaphore_wait(entered_z, 3)
+        post(dxs)
+    keep = pltpu.make_async_copy(packed.at[channel], arrived.at[me], local)
     keep.start()
 
-    for shift in SHIFTS:
-        there = shifted(*shift)
-        pltpu.make_async_remote_copy(
-            src_ref=packed.at[chip_index(*there)],
-            dst_ref=arrived.at[me],
-            send_sem=send,
-            recv_sem=recv,
-            device_id=device(*there, core),
-            device_id_type=MESH,
-        ).start()
-
     def gate_row(i, carry):
-        gating[i] = jax.nn.sigmoid(jnp.dot(normed[i], out_gate_w[...], preferred_element_type=F32))
+        gate = jnp.dot(normed[core, i], out_gate_w[...], preferred_element_type=F32)
+        gating[i] = 0.5 * jnp.tanh(0.5 * gate) + 0.5
         return carry
 
     lax.fori_loop(0, 40, gate_row, 0)
@@ -162,19 +206,29 @@
     )
     whole.wait_recv()
 
-    for g in range(7):
-        beside = [
-            jnp.concatenate([arrived[m * 8 + k, g * 16 : g * 16 + 16, :] for m in range(8)], axis=0)
-            for k in range(8)
-        ]
-        lanes = 1024 if g < 6 else 256
-        moved = jnp.dot(jnp.concatenate(beside, axis=1), swap[:, :lanes], preferred_element_type=F32).astype(BF16)
-        for s in range(8 if g < 6 else 2):
-            p = (g % 3) * 8 + s if g < 6 else 24
-            target = left if (g < 3 or (g == 6 and s == 0)) else right
+    def beside(rows):
+        return jnp.concatenate(
+            [jnp.concatenate([arrived[m * 8 + k, rows, :] for m in range(8)], axis=0) for k in range(8)], axis=1
+        )
+
+    for g in range(6):
+        moved = jnp.dot(beside(slice(g * 16, g * 16 + 16)), swap[...], preferred_element_type=F32).astype(BF16)
+        for s in range(8):
+            p = (g % 3) * 8 + s
+            target = left if g < 3 else right
             target[(p // 5) * 128 : (p // 5) * 128 + 128, (p % 5) * 128 : (p % 5) * 128 + 128] = (
                 moved[:, s * 128 : s * 128 + 128]
             )
+    moved = jnp.dot(beside(slice(96, 104)), swap[...], preferred_element_type=F32)
+    for n in range(8):
+        finished[n * 64 : n * 64 + 64, :] = moved[:, n * 128 : n * 128 + 128]
+        for side in range(2):
+            for h in range(2):
+                finished[pl.ds(512 + side * 128 + h * 8 + n, 8, stride=16), :] = finished[
+                    pl.ds(n * 64 + side * 2 + h, 8, stride=8), :
+                ]
+    left[512:640, 512:640] = finished[512:640, :].astype(BF16)
+    right[512:640, 512:640] = finished[640:768, :].astype(BF16)
 
     for n in range(5):
         rows = pl.ds(n * 128, 128)
@@ -200,7 +254,7 @@
                         tile, axis=0
                     ).astype(BF16)
 
-    mine = core * CHIPS + me
+    mine = core * CHIPS + channel
     keep_back = pltpu.make_async_copy(back.at[me * 2 + core], returned.at[mine], local)
     keep_back.start()
 
@@ -271,10 +325,10 @@
         in_specs=[pl.BlockSpec(memory_space=pltpu.VMEM)] * 10,
         out_specs=pl.BlockSpec(memory_space=pltpu.VMEM),
         scratch_shapes=[
-            pltpu.VMEM((40, 80, 128), BF16),
             pltpu.VMEM((2, 40, 80, 128), BF16),
+            pltpu.VMEM((2, 32, 128), F32),
             pltpu.VMEM((40, 80, 128), F32),
-            pltpu.VMEM((256, 128), BF16),
+            pltpu.VMEM((4, 64, 128), BF16),
             pltpu.VMEM((CHIPS * ROWS, 128), F32),
             pltpu.VMEM((CHIPS, ROWS, 128), BF16),
             pltpu.VMEM((CHIPS, ROWS, 128), BF16),
@@ -285,7 +339,7 @@
             pltpu.VMEM((2 * CHIPS, BACK, 128), BF16),
             pltpu.VMEM((2 * CHIPS, BACK, 128), BF16),
             pltpu.VMEM((128 * BACK, 128), F32),
-            dma, dma, dma, dma, dma, dma, dma, pltpu.SemaphoreType.REGULAR, pltpu.SemaphoreType.REGULAR,
+            pltpu.SemaphoreType.DMA((3,)), pltpu.SemaphoreType.DMA((3,)), dma, dma, dma, dma, dma, pltpu.SemaphoreType.REGULAR, pltpu.SemaphoreType.REGULAR,
         ],
         compiler_params=pltpu.CompilerParams(
             collective_id=0, has_side_effects=True, vmem_limit_bytes=56 * 2**20

time: 70.9 us -> 62.5 us (0.88)
  Pallas kernels: 68.6 us -> 60.3 us
    pallas_call x1, Pallas kernels: 68.6 us -> 60.3 us  [body(): pl.pallas_call(kernel, out_shape=jax.ShapeDtypeStruct(pair.shape, BF16),...]
where the time goes in v3:
time: 62.5 us; the launch traced here: 62.4 us
  Pallas kernels  60.3 us (96%)
  local copies, waits for them, and re-layouts  2.09 us (3%)
    pallas_call x1, Pallas kernels, body(): pl.pallas_call(kernel, out_shape=jax.ShapeDtypeStruct(pair.shape, BF16),...  60.3 us
    unnamed x1, local copies, waits for them, and re-layouts  2.09 us

profile of v3, /device:TPU:1, one launch (start us, length us, event | category | flops | bytes accessed | tf_op | source)
XLA Modules:
  0.0 62.4 jit_solution(17309146992060501622)
XLA Ops:
  0.0 60.3 %shard_map.100 = bf16[40,80,128]{2,1,0:T(8,128)(2,1)} custom-call(bf16[40,80,128]{2,1,0:T(8,128)(2,1)} %pair.1, s32[40,80]{1,0:T(8,128)} %mask.1, f32[1,128]{1,0:T(1,128)} %bitcast.4, f32[1,128]{1,0:T(1,128)} %bitcast.5, bf16[128,256]{1,0:T(8,128)(2,1)} %proj_w.1, bf16[128,256]{1,0:T(8,128)(2,1)} %gate_w.1, f32[1,128]{1,0:T(1,128)} %bitcast.6, ...), custom_call_target="tpu_custom_call" | custom-call | tf_op jit(solution)/shard_map/pallas_call | solution.py:322
  60.3 2.1 %copy.12 = bf16[40,80,128]{2,1,0:T(8,128)(2,1)} copy(bf16[40,80,128]{2,1,0:T(8,128)(2,1)} %shard_map.100) | data formatting | bytes 1638400

commit v4 on v3

v4 whole, which is shorter than its diff:
```python
import functools

import jax
import jax.numpy as jnp
from jax import lax
from jax.experimental import pallas as pl
from jax.experimental.pallas import tpu as pltpu
from jax.sharding import PartitionSpec as P

MESH = pl.DeviceIdType.MESH
F32, BF16 = jnp.float32, jnp.bfloat16
NT = (((1,), (1,)), ((), ()))
CHIPS = 64
ROWS = 104
BACK = 32


def device(x, y, z, core):
    return (y * 4 + (z // 2) * 2 + core, x * 2 + z % 2)


def chip_index(x, y, z):
    return (y * 2 + z // 2) * 8 + x * 2 + z % 2


def channel_of(x, y, z):
    return x * 16 + y * 4 + z


def distance(shift):
    return sum(min(d, 4 - d) for d in shift)


SHIFTS = sorted(
    [(n // 16, n // 4 % 4, n % 4) for n in range(1, CHIPS)],
    key=lambda s: (-distance(s), -min(s[1], 4 - s[1]), (s[0] * 7 + s[1] * 11 + s[2] * 13) % 16),
)


def kernel(
    pair, mask, norm_gain, norm_bias, proj_w, gate_w, out_gain, out_bias, out_w, out_gate_w,
    out,
    normed, masks, gating, weights, wide, packed, arrived, left, right, swap, combined, back_0, back_1,
    returned_0, returned_1, last_out, last_in, last_gating, finished,
    sibling_send, sibling_recv, send, recv, back_send, back_recv, last_send, last_recv, local, entered_y, entered_z,
):
    r, c = lax.axis_index("row"), lax.axis_index("col")
    x, y, z, core = c // 2, r // 4, ((r // 2) % 2) * 2 + c % 2, r % 2
    me, channel = chip_index(x, y, z), channel_of(x, y, z)

    def shifted(dx, dy, dz):
        return (x + dx) % 4, (y + dy) % 4, (z + dz) % 4

    barrier = pltpu.get_barrier_semaphore()
    sibling = device(x, y, z, 1 - core)
    along = [[device(*shifted(*(d * (a == n) for a in range(3))), core) for d in (1, 2, 3)] for n in range(3)]
    for there in [sibling] + along[0] + along[1] + along[2]:
        pl.semaphore_signal(barrier, inc=1, device_id=there, device_id_type=MESH)

    def pass_on(sem, line):
        for there in line:
            pl.semaphore_signal(sem, inc=1, device_id=there, device_id_type=MESH)

    lane = lax.broadcasted_iota(jnp.int32, (8, 128), 1)
    finished[0:40, 0:128] = jnp.zeros((40, 128), F32)
    finished[0:40, 0:80] = mask[...].astype(F32)
    for g in range(3):
        valid = jnp.zeros((8, 128), F32)
        for s in range(8):
            p = 8 * g + s
            turned = pltpu.roll(finished[p // 5 * 8 : p // 5 * 8 + 8, :], (s - p % 5) * 16 % 128, 1)
            valid = jnp.where(lane // 16 == s, turned, valid)
        masks[core, g * 8 : g * 8 + 8, :] = valid
    last = jnp.zeros((8, 128), F32)
    for n in range(8):
        turned = pltpu.roll(jnp.broadcast_to(finished[32 + n : 33 + n, :], (8, 128)), (n - 4) * 16 % 128, 1)
        last = jnp.where(lane // 16 == n, turned, last)
    masks[core, 24:32, :] = last

    gain, bias = norm_gain[...], norm_bias[...]

    def norm_rows(n, carry):
        values = pair[pl.ds(n * 4, 4)].astype(F32)
        mean = jnp.mean(values, axis=-1, keepdims=True)
        centred = values - mean
        var = jnp.mean(centred * centred, axis=-1, keepdims=True)
        normed[core, pl.ds(n * 4, 4)] = (centred * lax.rsqrt(var + 1e-05) * gain + bias).astype(BF16)
        return carry

    def to_sibling(ref, send_sem, recv_sem):
        return pltpu.make_async_remote_copy(
            src_ref=ref, dst_ref=ref, send_sem=send_sem, recv_sem=recv_sem, device_id=sibling, device_id_type=MESH
        )

    exchange = [
        to_sibling(masks.at[core], sibling_send.at[0], sibling_recv.at[0]),
        to_sibling(normed.at[core, pl.ds(0, 20)], sibling_send.at[1], sibling_recv.at[1]),
        to_sibling(normed.at[core, pl.ds(20, 20)], sibling_send.at[2], sibling_recv.at[2]),
    ]
    lax.fori_loop(0, 5, norm_rows, 0, unroll=5)
    pl.semaphore_wait(barrier, 10)
    exchange[0].start()
    exchange[1].start()
    pass_on(entered_y, along[1])
    lax.fori_loop(5, 10, norm_rows, 0, unroll=5)
    exchange[2].start()

    half = pl.ds(pl.multiple_of(core * 64, 64), 64)
    for n, w in enumerate((proj_w, gate_w)):
        for side in range(2):
            finished[0:128, :] = jnp.transpose(w[:, side * 128 : side * 128 + 128].astype(F32))
            weights[(n * 2 + side) * 64 : (n * 2 + side) * 64 + 64, :] = finished[half, :].astype(BF16)

    def project(who):
        def values_of(tokens, valid):
            got = lax.dot_general(weights[...], tokens, NT, preferred_element_type=F32)
            return got[:128] * (0.5 * jnp.tanh(0.5 * got[128:]) + 0.5) * valid

        def put(values, row, side_rows):
            for side in range(2):
                wide[pl.ds(side * side_rows + row, CHIPS, stride=ROWS), :] = values[side * 64 : side * 64 + 64]

        def project_row(inner, carry):
            tokens = [
                normed[who, (p // 5) * 8 + inner, (p % 5) * 16 : (p % 5) * 16 + 16, :] for p in range(24)
            ]
            valid = jnp.concatenate([masks[who, pl.ds(g * 8 + inner, 1), :] for g in range(3)], axis=1)
            values = values_of(jnp.concatenate(tokens, axis=0), valid)
            for g in range(3):
                put(values[:, g * 128 : g * 128 + 128], g * 16 + who * 8 + inner, 48)
            return carry

        lax.fori_loop(0, 8, project_row, 0, unroll=8)
        last_tokens = [normed[who, 32 + n, 64:80, :] for n in range(8)]
        put(values_of(jnp.concatenate(last_tokens, axis=0), masks[who, 24:25, :]), 96 + who, 2)

    for row in range(100, ROWS):
        wide[pl.ds(row, CHIPS, stride=ROWS), :] = jnp.zeros((CHIPS, 128), F32)
    project(core)
    pl.semaphore_wait(entered_y, 3)
    pass_on(entered_z, along[2])
    for e in exchange:
        e.wait()
    project(1 - core)

    def narrow(m, carry):
        packed[m] = wide[pl.ds(pl.multiple_of(m * ROWS, 8), ROWS), :].astype(BF16)
        return carry

    lax.fori_loop(0, CHIPS, narrow, 0, unroll=4)
    pl.semaphore_wait(entered_z, 3)
    for shift in SHIFTS:
        there = shifted(*shift)
        pltpu.make_async_remote_copy(
            src_ref=packed.at[channel_of(*there)],
            dst_ref=arrived.at[me],
            send_sem=send,
            recv_sem=recv.at[shift[1]],
            device_id=device(*there, core),
            device_id_type=MESH,
        ).start()
    keep = pltpu.make_async_copy(packed.at[channel], arrived.at[me], local)
    keep.start()

    def gate_row(i, carry):
        gate = jnp.dot(normed[core, i], out_gate_w[...], preferred_element_type=F32)
        gating[i] = 0.5 * jnp.tanh(0.5 * gate) + 0.5
        return carry

    lax.fori_loop(0, 40, gate_row, 0)
    for inner in range(8):
        tokens = jnp.concatenate([normed[1, 32 + inner, h * 40 + 32 : h * 40 + 40, :] for h in range(2)], axis=0)
        gate = jnp.dot(tokens, out_gate_w[...], preferred_element_type=F32)
        last_gating[inner] = 0.5 * jnp.tanh(0.5 * gate) + 0.5
    for a in range(8):
        at = lax.broadcasted_iota(jnp.int32, (128, 1024), 0)
        to = lax.broadcasted_iota(jnp.int32, (128, 1024), 1)
        swap[a * 128 : a * 128 + 128, :] = (to == (at // 16) * 128 + a * 16 + at % 16).astype(F32).astype(BF16)
    w_t = jnp.transpose(out_w[...].astype(F32))
    offset = lax.dot_general(out_bias[...], w_t, NT, preferred_element_type=F32, precision=lax.Precision.HIGHEST)
    scaled = jnp.transpose(w_t * out_gain[...]).astype(BF16)

    for dy in (2, 1, 3, 0):
        n_from = 16 if dy else 15
        pltpu.make_async_remote_copy(
            src_ref=packed.at[pl.ds(0, n_from)],
            dst_ref=arrived.at[pl.ds(0, n_from)],
            send_sem=send,
            recv_sem=recv.at[dy],
            device_id=sibling,
            device_id_type=MESH,
        ).wait_recv()
        if dy == 0:
            keep.wait()
        first = (y + 4 - dy) % 4 * 2
        beside = [
            jnp.concatenate([arrived[(first + m) * 8 + k] for m in range(2)], axis=0) for k in range(8)
        ]
        moved = jnp.dot(jnp.concatenate(beside, axis=1), swap[...], preferred_element_type=F32)
        for m in range(2):
            for side, target in enumerate((left, right)):
                for p in range(24):
                    row, col = m * ROWS + side * 48 + p // 8 * 16, p % 8 * 128
                    at = pl.ds(pl.multiple_of(p // 5 * 128 + (first + m) * 16, 16), 16)
                    target[at, p % 5 * 128 : p % 5 * 128 + 128] = moved[row : row + 16, col : col + 128].astype(BF16)
                for n in range(16):
                    row = m * ROWS + 96 + side * 2 + n // 8
                    finished[n : n + 1, :] = moved[row : row + 1, n % 8 * 128 : n % 8 * 128 + 128]
                at = pl.ds(pl.multiple_of(512 + (first + m) * 16, 16), 16)
                target[at, 512:640] = finished[0:16, :].astype(BF16)

    for n in range(5):
        rows = pl.ds(n * 128, 128)
        got = lax.dot_general(left[rows, :], right[...], NT, preferred_element_type=F32)
        combined[rows, :] = got.astype(BF16)
        if n == 4:
            turned = [got[m * 16 + h : m * 16 + h + 8, 512:640] for m in range(8) for h in (8, 0)]
            last_turned = jnp.concatenate(turned, axis=0).astype(BF16)

    moved = []
    for g in range(4):
        blocks = [
            combined[p // 5 * 128 : p // 5 * 128 + 128, p % 5 * 128 : p % 5 * 128 + 128]
            for p in range(8 * g, min(8 * g + 8, 25))
        ] + ([last_turned] if g == 3 else [])
        moved.append(
            jnp.dot(jnp.concatenate(blocks, axis=1), swap[: 128 * len(blocks), :], preferred_element_type=F32)
        )
    for m in range(8):
        for k in range(8):
            for h, (target, groups) in enumerate(((back_0, 4), (back_1, 3))):
                row = m * 16 + h * 8
                tiles = [v[row : row + 8, k * 128 : k * 128 + 128] for v in moved[:groups]]
                target[m * 8 + k] = jnp.concatenate(tiles, axis=0).astype(BF16)

    mine = core * CHIPS + channel
    sides = ((back_0, returned_0, back_send.at[0], back_recv.at[0]), (back_1, returned_1, back_send.at[1], back_recv.at[1]))

    for shift in SHIFTS:
        there = shifted(*shift)
        for to_core, (source, target, send_sem, recv_sem) in enumerate(sides):
            pltpu.make_async_remote_copy(
                src_ref=source.at[chip_index(*there)],
                dst_ref=target.at[mine],
                send_sem=send_sem,
                recv_sem=recv_sem,
                device_id=device(*there, to_core),
                device_id_type=MESH,
            ).start()

    def end(own):
        source, target, send_sem, recv_sem = sides[own]
        other_source, other_target, other_send, other_recv = sides[1 - own]
        groups = 4 - own
        pltpu.make_async_remote_copy(
            src_ref=other_source.at[me],
            dst_ref=other_target.at[mine],
            send_sem=other_send,
            recv_sem=other_recv,
            device_id=sibling,
            device_id_type=MESH,
        ).start()
        keep_back = pltpu.make_async_copy(source.at[me], target.at[mine], local)
        keep_back.start()
        keep_back.wait()

        def whole(refs, sems, n):
            return pltpu.make_async_remote_copy(
                src_ref=refs[0].at[pl.ds(0, n)],
                dst_ref=refs[1].at[pl.ds(0, n)],
                send_sem=sems[0],
                recv_sem=sems[1],
                device_id=sibling,
                device_id_type=MESH,
            )

        whole((target, target), (send_sem, recv_sem), 2 * CHIPS - 1).wait_recv()

        def total(ch, carry):
            return carry + target[ch].astype(F32)

        none = jnp.zeros((groups * 8, 128), F32)
        mean = lax.fori_loop(0, 128, total, none, unroll=16) * (1 / 128)

        def spread(ch, carry):
            centred = target[ch].astype(F32) - mean
            return carry + centred * centred

        var = lax.fori_loop(0, 128, spread, none, unroll=16) * (1 / 128)
        scale = lax.rsqrt(var + 1e-05)

        def normalise(ch, carry):
            finished[pl.ds(pl.multiple_of(ch * BACK, BACK), groups * 8), :] = (target[ch].astype(F32) - mean) * scale
            return carry

        lax.fori_loop(0, 128, normalise, 0, unroll=16)

        def projected(row, n_blocks):
            values = finished[pl.ds(row, 128, stride=BACK), :]
            tokens = jnp.transpose(values)[: 16 * n_blocks, :].astype(BF16)
            return jnp.dot(tokens, scaled, preferred_element_type=F32) + offset

        def put(got, inner, p, s):
            at = p // 5 * 8 + inner
            for h in range(2):
                cols = pl.ds(h * 40 + p % 5 * 8, 8)
                rows = got[s * 16 + h * 8 : s * 16 + h * 8 + 8, :]
                out[at, cols, :] = (rows * gating[at, cols, :]).astype(BF16)

        passed = pltpu.make_async_remote_copy(
            src_ref=last_out,
            dst_ref=last_in,
            send_sem=last_send,
            recv_sem=last_recv,
            device_id=sibling,
            device_id_type=MESH,
        )
        if own == 0:

            def last_row(inner, carry):
                got = projected(24 + inner, 2)
                put(got, inner, 24, 0)
                last_out[inner] = (got[16:32, :] * last_gating[inner]).astype(BF16)
                return carry

            lax.fori_loop(0, 8, last_row, 0, unroll=8)
            passed.start()

        def finish(inner, carry):
            for g in range(3):
                got = projected(g * 8 + inner, 8)
                for s in range(8):
                    put(got, inner, 8 * g + s, s)
            return carry

        lax.fori_loop(0, 8, finish, 0, unroll=4)
        if own == 0:
            passed.wait_send()
        else:
            passed.wait_recv()
            for inner in range(8):
                for h in range(2):
                    out[32 + inner, pl.ds(h * 40 + 32, 8), :] = last_in[inner, h * 8 : h * 8 + 8, :]
        whole((source, source), (send_sem, recv_sem), CHIPS - 1).wait_send()
        whole((other_source, other_source), (other_send, other_recv), CHIPS).wait_send()

    pl.when(core == 0)(functools.partial(end, 0))
    pl.when(core == 1)(functools.partial(end, 1))
    pltpu.make_async_remote_copy(
        src_ref=packed.at[pl.ds(0, CHIPS - 1)],
        dst_ref=arrived.at[pl.ds(0, CHIPS - 1)],
        send_sem=send,
        recv_sem=recv.at[0],
        device_id=sibling,
        device_id_type=MESH,
    ).wait_send()


def body(*args):
    pair, mask, norm_gain, norm_bias, proj_w, gate_w, out_gain, out_bias, out_w, out_gate_w = args
    dma = pltpu.SemaphoreType.DMA
    return pl.pallas_call(
        kernel,
        out_shape=jax.ShapeDtypeStruct(pair.shape, BF16),
        in_specs=[pl.BlockSpec(memory_space=pltpu.VMEM)] * 10,
        out_specs=pl.BlockSpec(memory_space=pltpu.VMEM),
        scratch_shapes=[
            pltpu.VMEM((2, 40, 80, 128), BF16),
            pltpu.VMEM((2, 32, 128), F32),
            pltpu.VMEM((40, 80, 128), F32),
            pltpu.VMEM((256, 128), BF16),
            pltpu.VMEM((CHIPS * ROWS, 128), F32),
            pltpu.VMEM((CHIPS, ROWS, 128), BF16),
            pltpu.VMEM((CHIPS, ROWS, 128), BF16),
            pltpu.VMEM((640, 640), BF16),
            pltpu.VMEM((640, 640), BF16),
            pltpu.VMEM((1024, 1024), BF16),
            pltpu.VMEM((640, 640), BF16),
            pltpu.VMEM((CHIPS, BACK, 128), BF16),
            pltpu.VMEM((CHIPS, BACK - 8, 128), BF16),
            pltpu.VMEM((2 * CHIPS, BACK, 128), BF16),
            pltpu.VMEM((2 * CHIPS, BACK - 8, 128), BF16),
            pltpu.VMEM((8, 16, 128), BF16),
            pltpu.VMEM((8, 16, 128), BF16),
            pltpu.VMEM((8, 16, 128), F32),
            pltpu.VMEM((128 * BACK, 128), F32),
            dma((3,)), dma((3,)), dma, dma((4,)), dma((2,)), dma((2,)), dma, dma, dma, pltpu.SemaphoreType.REGULAR, pltpu.SemaphoreType.REGULAR,
        ],
        compiler_params=pltpu.CompilerParams(
            collective_id=0, has_side_effects=True, vmem_limit_bytes=56 * 2**20
        ),
    )(
        pair, mask, norm_gain.reshape(1, 128), norm_bias.reshape(1, 128), proj_w, gate_w,
        out_gain.reshape(1, 128), out_bias.reshape(1, 128), out_w, out_gate_w,
    )


def solution(mesh):
    placed = (P("row", "col", None), P("row", "col"), P(), P(), P(), P(), P(), P(), P(), P())
    return jax.shard_map(body, mesh=mesh, in_specs=placed, out_specs=P("row", "col", None), check_vma=False)
```

time: 62.5 us -> 56.6 us (0.906)
  Pallas kernels: 60.3 us -> 54.3 us
    pallas_call x1, Pallas kernels: 60.3 us -> 54.3 us  [body(): pl.pallas_call(kernel, out_shape=jax.ShapeDtypeStruct(pair.shape, BF16),...]
where the time goes in v4:
time: 56.6 us; the launch traced here: 56.4 us
  Pallas kernels  54.3 us (96%)
  local copies, waits for them, and re-layouts  2.09 us (4%)
    pallas_call x1, Pallas kernels, body(): pl.pallas_call(kernel, out_shape=jax.ShapeDtypeStruct(pair.shape, BF16),...  54.3 us
    unnamed x1, local copies, waits for them, and re-layouts  2.09 us

profile of v4, /device:TPU:1, one launch (start us, length us, event | category | flops | bytes accessed | tf_op | source)
XLA Modules:
  0.0 56.4 jit_solution(8644310445852693141)
XLA Ops:
  0.0 54.3 %shard_map.100 = bf16[40,80,128]{2,1,0:T(8,128)(2,1)} custom-call(bf16[40,80,128]{2,1,0:T(8,128)(2,1)} %pair.1, s32[40,80]{1,0:T(8,128)} %mask.1, f32[1,128]{1,0:T(1,128)} %bitcast.4, f32[1,128]{1,0:T(1,128)} %bitcast.5, bf16[128,256]{1,0:T(8,128)(2,1)} %proj_w.1, bf16[128,256]{1,0:T(8,128)(2,1)} %gate_w.1, f32[1,128]{1,0:T(1,128)} %bitcast.6, ...), custom_call_target="tpu_custom_call" | custom-call | tf_op jit(solution)/shard_map/pallas_call | solution.py:362
  54.3 2.1 %copy.12 = bf16[40,80,128]{2,1,0:T(8,128)(2,1)} copy(bf16[40,80,128]{2,1,0:T(8,128)(2,1)} %shard_map.100) | data formatting | bytes 1638400

commit v5 on v4

--- a/solution.py
+++ b/solution.py
@@ -101,7 +101,7 @@
     pl.semaphore_wait(barrier, 10)
     exchange[0].start()
     exchange[1].start()
-    pass_on(entered_y, along[1])
+    pass_on(entered_y, along[0] + along[1] + along[2])
     lax.fori_loop(5, 10, norm_rows, 0, unroll=5)
     exchange[2].start()
 
@@ -137,7 +137,7 @@
     for row in range(100, ROWS):
         wide[pl.ds(row, CHIPS, stride=ROWS), :] = jnp.zeros((CHIPS, 128), F32)
     project(core)
-    pl.semaphore_wait(entered_y, 3)
+    pl.semaphore_wait(entered_y, 9)
     pass_on(entered_z, along[2])
     for e in exchange:
         e.wait()
@@ -148,17 +148,23 @@
         return carry
 
     lax.fori_loop(0, CHIPS, narrow, 0, unroll=4)
+
+    def post(shifts):
+        for shift in shifts:
+            there = shifted(*shift)
+            pltpu.make_async_remote_copy(
+                src_ref=packed.at[channel_of(*there)],
+                dst_ref=arrived.at[me],
+                send_sem=send,
+                recv_sem=recv.at[shift[1]],
+                device_id=device(*there, core),
+                device_id_type=MESH,
+            ).start()
+
+    early = [s for s in SHIFTS if 0 in s and distance(s) > 2]
+    post(early)
     pl.semaphore_wait(entered_z, 3)
-    for shift in SHIFTS:
-        there = shifted(*shift)
-        pltpu.make_async_remote_copy(
-            src_ref=packed.at[channel_of(*there)],
-            dst_ref=arrived.at[me],
-            send_sem=send,
-            recv_sem=recv.at[shift[1]],
-            device_id=device(*there, core),
-            device_id_type=MESH,
-        ).start()
+    post([s for s in SHIFTS if s not in early])
     keep = pltpu.make_async_copy(packed.at[channel], arrived.at[me], local)
     keep.start()
 
@@ -361,7 +367,7 @@
     dma = pltpu.SemaphoreType.DMA
     return pl.pallas_call(
         kernel,
-        out_shape=jax.ShapeDtypeStruct(pair.shape, BF16),
+        out_shape=pltpu.VMEM(pair.shape, BF16),
         in_specs=[pl.BlockSpec(memory_space=pltpu.VMEM)] * 10,
         out_specs=pl.BlockSpec(memory_space=pltpu.VMEM),
         scratch_shapes=[

time: 56.6 us -> 54.3 us (0.959)
  local copies, waits for them, and re-layouts: 2.09 us -> 0.89 us
  Pallas kernels: 54.3 us -> 53.3 us
    unnamed x1, local copies, waits for them, and re-layouts: 2.09 us -> 0.89 us
    pallas_call x1, Pallas kernels: 54.3 us -> 53.3 us  [body(): pl.pallas_call(kernel, out_shape=pltpu.VMEM(pair.shape, BF16), in_specs=[...]
where the time goes in v5:
time: 54.3 us; the launch traced here: 54.2 us
  Pallas kernels  53.3 us (98%)
  local copies, waits for them, and re-layouts  0.89 us (2%)
    pallas_call x1, Pallas kernels, body(): pl.pallas_call(kernel, out_shape=pltpu.VMEM(pair.shape, BF16), in_specs=[...  53.3 us

profile of v5, /device:TPU:1, one launch (start us, length us, event | category | flops | bytes accessed | tf_op | source)
XLA Modules:
  0.0 54.2 jit_solution(9407746792443285695)
XLA Ops:
  0.0 53.3 %shard_map.100 = bf16[40,80,128]{2,1,0:T(8,128)(2,1)S(1)} custom-call(bf16[40,80,128]{2,1,0:T(8,128)(2,1)} %pair.1, s32[40,80]{1,0:T(8,128)} %mask.1, f32[1,128]{1,0:T(1,128)} %bitcast.4, f32[1,128]{1,0:T(1,128)} %bitcast.5, bf16[128,256]{1,0:T(8,128)(2,1)} %proj_w.1, bf16[128,256]{1,0:T(8,128)(2,1)} %gate_w.1, f32[1,128]{1,0:T(1,128)} %bitcast.6, ...), custom_call_target="tpu_custom_call" | custom-call | tf_op jit(solution)/shard_map/pallas_call | solution.py:368
  53.3 0.9 %copy.12 = bf16[40,80,128]{2,1,0:T(8,128)(2,1)} copy(bf16[40,80,128]{2,1,0:T(8,128)(2,1)S(1)} %shard_map.100) | data formatting | bytes 1638400

commit v6 on v5

--- a/solution.py
+++ b/solution.py
@@ -38,8 +38,9 @@
 
 
 def kernel(
-    pair, mask, norm_gain, norm_bias, proj_w, gate_w, out_gain, out_bias, out_w, out_gate_w,
+    pair_in, mask_in, norm_gain_in, norm_bias_in, proj_w_in, gate_w_in, out_gain_in, out_bias_in, out_w_in, out_gate_w_in,
     out,
+    pair, mask, norm_gain, norm_bias, proj_w, gate_w, out_gain, out_bias, out_w, out_gate_w, load,
     normed, masks, gating, weights, wide, packed, arrived, left, right, swap, combined, back_0, back_1,
     returned_0, returned_1, last_out, last_in, last_gating, finished,
     sibling_send, sibling_recv, send, recv, back_send, back_recv, last_send, last_recv, local, entered_y, entered_z,
@@ -60,6 +61,15 @@
     def pass_on(sem, line):
         for there in line:
             pl.semaphore_signal(sem, inc=1, device_id=there, device_id_type=MESH)
+
+    sources = (
+        pair_in, mask_in, norm_gain_in, norm_bias_in, proj_w_in, gate_w_in, out_gain_in, out_bias_in, out_w_in, out_gate_w_in
+    )
+    places = (pair, mask, norm_gain, norm_bias, proj_w, gate_w, out_gain, out_bias, out_w, out_gate_w)
+    loads = [pltpu.make_async_copy(a, b, load.at[n]) for n, (a, b) in enumerate(zip(sources, places))]
+    for n in (1, 0, 2, 3, 4, 5, 6, 7, 8, 9):
+        loads[n].start()
+    loads[1].wait()
 
     lane = lax.broadcasted_iota(jnp.int32, (8, 128), 1)
     finished[0:40, 0:128] = jnp.zeros((40, 128), F32)
@@ -77,6 +87,8 @@
         last = jnp.where(lane // 16 == n, turned, last)
     masks[core, 24:32, :] = last
 
+    for n in (0, 2, 3):
+        loads[n].wait()
     gain, bias = norm_gain[...], norm_bias[...]
 
     def norm_rows(n, carry):
@@ -105,6 +117,8 @@
     lax.fori_loop(5, 10, norm_rows, 0, unroll=5)
     exchange[2].start()
 
+    for n in (4, 5, 6, 7, 8, 9):
+        loads[n].wait()
     half = pl.ds(pl.multiple_of(core * 64, 64), 64)
     for n, w in enumerate((proj_w, gate_w)):
         for side in range(2):
@@ -215,23 +229,19 @@
                 at = pl.ds(pl.multiple_of(512 + (first + m) * 16, 16), 16)
                 target[at, 512:640] = finished[0:16, :].astype(BF16)
 
-    for n in range(5):
-        rows = pl.ds(n * 128, 128)
-        got = lax.dot_general(left[rows, :], right[...], NT, preferred_element_type=F32)
-        combined[rows, :] = got.astype(BF16)
-        if n == 4:
-            turned = [got[m * 16 + h : m * 16 + h + 8, 512:640] for m in range(8) for h in (8, 0)]
-            last_turned = jnp.concatenate(turned, axis=0).astype(BF16)
-
-    moved = []
-    for g in range(4):
-        blocks = [
-            combined[p // 5 * 128 : p // 5 * 128 + 128, p % 5 * 128 : p % 5 * 128 + 128]
-            for p in range(8 * g, min(8 * g + 8, 25))
-        ] + ([last_turned] if g == 3 else [])
-        moved.append(
-            jnp.dot(jnp.concatenate(blocks, axis=1), swap[: 128 * len(blocks), :], preferred_element_type=F32)
-        )
+    got = lax.dot_general(left[...], right[...], NT, preferred_element_type=F32)
+    combined[...] = got.astype(BF16)
+    turned = [got[512 + m * 16 + h : 512 + m * 16 + h + 8, 512:640] for m in range(8) for h in (8, 0)]
+    last_turned = jnp.concatenate(turned, axis=0).astype(BF16)
+
+    def block(p):
+        return combined[p // 5 * 128 : p // 5 * 128 + 128, p % 5 * 128 : p % 5 * 128 + 128]
+
+    groups = [jnp.concatenate([block(p) for p in range(8 * g, 8 * g + 8)], axis=1) for g in range(3)]
+    moved_3 = jnp.dot(jnp.concatenate(groups, axis=0), swap[...], preferred_element_type=F32)
+    last = jnp.concatenate([block(24), last_turned], axis=1)
+    moved = [moved_3[g * 128 : g * 128 + 128] for g in range(3)]
+    moved.append(jnp.dot(last, swap[0:256, :], preferred_element_type=F32))
     for m in range(8):
         for k in range(8):
             for h, (target, groups) in enumerate(((back_0, 4), (back_1, 3))):
@@ -364,13 +374,19 @@
 
 def body(*args):
     pair, mask, norm_gain, norm_bias, proj_w, gate_w, out_gain, out_bias, out_w, out_gate_w = args
+    operands = (
+        pair, mask, norm_gain.reshape(1, 128), norm_bias.reshape(1, 128), proj_w, gate_w,
+        out_gain.reshape(1, 128), out_bias.reshape(1, 128), out_w, out_gate_w,
+    )
     dma = pltpu.SemaphoreType.DMA
     return pl.pallas_call(
         kernel,
         out_shape=pltpu.VMEM(pair.shape, BF16),
-        in_specs=[pl.BlockSpec(memory_space=pltpu.VMEM)] * 10,
+        in_specs=[pl.BlockSpec(memory_space=pl.ANY)] * 10,
         out_specs=pl.BlockSpec(memory_space=pltpu.VMEM),
-        scratch_shapes=[
+        scratch_shapes=[pltpu.VMEM(a.shape, a.dtype) for a in operands]
+        + [
+            dma((10,)),
             pltpu.VMEM((2, 40, 80, 128), BF16),
             pltpu.VMEM((2, 32, 128), F32),
             pltpu.VMEM((40, 80, 128), F32),
@@ -395,10 +411,7 @@
         compiler_params=pltpu.CompilerParams(
             collective_id=0, has_side_effects=True, vmem_limit_bytes=56 * 2**20
         ),
-    )(
-        pair, mask, norm_gain.reshape(1, 128), norm_bias.reshape(1, 128), proj_w, gate_w,
-        out_gain.reshape(1, 128), out_bias.reshape(1, 128), out_w, out_gate_w,
-    )
+    )(*operands)
 
 
 def solution(mesh):

time: 54.3 us -> 52.7 us (0.971)
  Pallas kernels: 53.3 us -> 51.6 us
    pallas_call x1, Pallas kernels: 53.3 us -> 51.6 us  [body(): pl.pallas_call(kernel, out_shape=pltpu.VMEM(pair.shape, BF16), in_specs=[...]
where the time goes in v6:
time: 52.7 us; the launch traced here: 52.5 us
  Pallas kernels  51.6 us (98%)
  local copies, waits for them, and re-layouts  0.89 us (2%)
    pallas_call x1, Pallas kernels, body(): pl.pallas_call(kernel, out_shape=pltpu.VMEM(pair.shape, BF16), in_specs=[...  51.6 us

profile of v6, /device:TPU:1, one launch (start us, length us, event | category | flops | bytes accessed | tf_op | source)
XLA Modules:
  0.0 52.5 jit_solution(17819357071253517464)
XLA Ops:
  0.0 51.6 %shard_map.100 = bf16[40,80,128]{2,1,0:T(8,128)(2,1)S(1)} custom-call(bf16[40,80,128]{2,1,0:T(8,128)(2,1)} %pair_in.1, s32[40,80]{1,0:T(8,128)} %mask_in.1, f32[1,128]{1,0:T(1,128)} %bitcast.4, f32[1,128]{1,0:T(1,128)} %bitcast.5, bf16[128,256]{1,0:T(8,128)(2,1)} %proj_w_in.1, bf16[128,256]{1,0:T(8,128)(2,1)} %gate_w_in.1, f32[1,128]{1,0:T(1,128)} %bitcast.6, ...), custom_call_target="tpu_custom_call" | custom-call | tf_op jit(solution)/shard_map/pallas_call | solution.py:382
  51.6 0.9 %copy.12 = bf16[40,80,128]{2,1,0:T(8,128)(2,1)} copy(bf16[40,80,128]{2,1,0:T(8,128)(2,1)S(1)} %shard_map.100) | data formatting | bytes 1638400

commit v7 on v6

--- a/solution.py
+++ b/solution.py
@@ -296,13 +296,16 @@
             return carry + target[ch].astype(F32)
 
         none = jnp.zeros((groups * 8, 128), F32)
-        mean = lax.fori_loop(0, 128, total, none, unroll=16) * (1 / 128)
-
-        def spread(ch, carry):
-            centred = target[ch].astype(F32) - mean
-            return carry + centred * centred
-
-        var = lax.fori_loop(0, 128, spread, none, unroll=16) * (1 / 128)
+        middle = lax.fori_loop(0, 32, total, none, unroll=16) * (1 / 32)
+
+        def spread(ch, sums):
+            centred = target[ch].astype(F32) - middle
+            return sums[0] + centred, sums[1] + centred * centred
+
+        moved_by, var = lax.fori_loop(0, 128, spread, (none, none), unroll=16)
+        moved_by = moved_by * (1 / 128)
+        mean = middle + moved_by
+        var = jnp.maximum(var * (1 / 128) - moved_by * moved_by, 0.0)
         scale = lax.rsqrt(var + 1e-05)
 
         def normalise(ch, carry):
@@ -391,7 +394,7 @@
             pltpu.VMEM((2, 32, 128), F32),
             pltpu.VMEM((40, 80, 128), F32),
             pltpu.VMEM((256, 128), BF16),
-            pltpu.VMEM((CHIPS * ROWS, 128), F32),
+            pltpu.VMEM((CHIPS * ROWS + ROWS, 128), F32),
             pltpu.VMEM((CHIPS, ROWS, 128), BF16),
             pltpu.VMEM((CHIPS, ROWS, 128), BF16),
             pltpu.VMEM((640, 640), BF16),
@@ -405,7 +408,7 @@
             pltpu.VMEM((8, 16, 128), BF16),
             pltpu.VMEM((8, 16, 128), BF16),
             pltpu.VMEM((8, 16, 128), F32),
-            pltpu.VMEM((128 * BACK, 128), F32),
+            pltpu.VMEM((128 * BACK + BACK, 128), F32),
             dma((3,)), dma((3,)), dma, dma((4,)), dma((2,)), dma((2,)), dma, dma, dma, pltpu.SemaphoreType.REGULAR, pltpu.SemaphoreType.REGULAR,
         ],
         compiler_params=pltpu.CompilerParams(

time: 52.7 us -> 52.6 us (level)
  no operation moved by 1% of the time
where the time goes in v7:
time: 52.6 us; the launch traced here: 52.5 us
  Pallas kernels  51.6 us (98%)
  local copies, waits for them, and re-layouts  0.89 us (2%)
    pallas_call x1, Pallas kernels, body(): pl.pallas_call(kernel, out_shape=pltpu.VMEM(pair.shape, BF16), in_specs=[...  51.6 us

profile of v7, /device:TPU:1, one launch (start us, length us, event | category | flops | bytes accessed | tf_op | source)
XLA Modules:
  0.0 52.5 jit_solution(9270296919634964784)
XLA Ops:
  0.0 51.6 %shard_map.100 = bf16[40,80,128]{2,1,0:T(8,128)(2,1)S(1)} custom-call(bf16[40,80,128]{2,1,0:T(8,128)(2,1)} %pair_in.1, s32[40,80]{1,0:T(8,128)} %mask_in.1, f32[1,128]{1,0:T(1,128)} %bitcast.4, f32[1,128]{1,0:T(1,128)} %bitcast.5, bf16[128,256]{1,0:T(8,128)(2,1)} %proj_w_in.1, bf16[128,256]{1,0:T(8,128)(2,1)} %gate_w_in.1, f32[1,128]{1,0:T(1,128)} %bitcast.6, ...), custom_call_target="tpu_custom_call" | custom-call | tf_op jit(solution)/shard_map/pallas_call | solution.py:385
  51.6 0.9 %copy.12 = bf16[40,80,128]{2,1,0:T(8,128)(2,1)} copy(bf16[40,80,128]{2,1,0:T(8,128)(2,1)S(1)} %shard_map.100) | data formatting | bytes 1638400

commit v8 on v7

--- a/solution.py
+++ b/solution.py
@@ -33,7 +33,7 @@
 
 SHIFTS = sorted(
     [(n // 16, n // 4 % 4, n % 4) for n in range(1, CHIPS)],
-    key=lambda s: (-distance(s), -min(s[1], 4 - s[1]), (s[0] * 7 + s[1] * 11 + s[2] * 13) % 16),
+    key=lambda s: (-max(distance(s), 2), -min(s[1], 4 - s[1]), -distance(s), (s[0] * 7 + s[1] * 11 + s[2] * 13) % 16),
 )
 
 
@@ -316,8 +316,8 @@
 
         def projected(row, n_blocks):
             values = finished[pl.ds(row, 128, stride=BACK), :]
-            tokens = jnp.transpose(values)[: 16 * n_blocks, :].astype(BF16)
-            return jnp.dot(tokens, scaled, preferred_element_type=F32) + offset
+            got = lax.dot_general(values.astype(BF16), scaled, (((0,), (0,)), ((), ())), preferred_element_type=F32)
+            return got[: 16 * n_blocks] + offset
 
         def put(got, inner, p, s):
             at = p // 5 * 8 + inner
@@ -352,7 +352,7 @@
                     put(got, inner, 8 * g + s, s)
             return carry
 
-        lax.fori_loop(0, 8, finish, 0, unroll=4)
+        lax.fori_loop(0, 8, finish, 0, unroll=8)
         if own == 0:
             passed.wait_send()
         else:

time: 52.6 us -> 52.6 us (level)
  no operation moved by 1% of the time
where the time goes in v8:
time: 52.6 us; the launch traced here: 52.5 us
  Pallas kernels  51.6 us (98%)
  local copies, waits for them, and re-layouts  0.89 us (2%)
    pallas_call x1, Pallas kernels, body(): pl.pallas_call(kernel, out_shape=pltpu.VMEM(pair.shape, BF16), in_specs=[...  51.6 us

profile of v8, /device:TPU:1, one launch (start us, length us, event | category | flops | bytes accessed | tf_op | source)
XLA Modules:
  0.0 52.5 jit_solution(17728569184475593673)
XLA Ops:
  0.0 51.6 %shard_map.100 = bf16[40,80,128]{2,1,0:T(8,128)(2,1)S(1)} custom-call(bf16[40,80,128]{2,1,0:T(8,128)(2,1)} %pair_in.1, s32[40,80]{1,0:T(8,128)} %mask_in.1, f32[1,128]{1,0:T(1,128)} %bitcast.4, f32[1,128]{1,0:T(1,128)} %bitcast.5, bf16[128,256]{1,0:T(8,128)(2,1)} %proj_w_in.1, bf16[128,256]{1,0:T(8,128)(2,1)} %gate_w_in.1, f32[1,128]{1,0:T(1,128)} %bitcast.6, ...), custom_call_target="tpu_custom_call" | custom-call | tf_op jit(solution)/shard_map/pallas_call | solution.py:385
  51.6 0.9 %copy.12 = bf16[40,80,128]{2,1,0:T(8,128)(2,1)} copy(bf16[40,80,128]{2,1,0:T(8,128)(2,1)S(1)} %shard_map.100) | data formatting | bytes 1638400

commit v9 on v8

--- a/solution.py
+++ b/solution.py
@@ -252,7 +252,7 @@
     mine = core * CHIPS + channel
     sides = ((back_0, returned_0, back_send.at[0], back_recv.at[0]), (back_1, returned_1, back_send.at[1], back_recv.at[1]))
 
-    for shift in SHIFTS:
+    for shift in sorted(SHIFTS, key=lambda s: (-distance(s), (s[0] * 7 + s[1] * 11 + s[2] * 13) % 16)):
         there = shifted(*shift)
         for to_core, (source, target, send_sem, recv_sem) in enumerate(sides):
             pltpu.make_async_remote_copy(

time: 52.6 us -> 52.5 us (level)
  no operation moved by 1% of the time
where the time goes in v9:
time: 52.5 us; the launch traced here: 52.4 us
  Pallas kernels  51.5 us (98%)
  local copies, waits for them, and re-layouts  0.89 us (2%)
    pallas_call x1, Pallas kernels, body(): pl.pallas_call(kernel, out_shape=pltpu.VMEM(pair.shape, BF16), in_specs=[...  51.5 us

profile of v9, /device:TPU:1, one launch (start us, length us, event | category | flops | bytes accessed | tf_op | source)
XLA Modules:
  0.0 52.4 jit_solution(11359293867247779707)
XLA Ops:
  0.0 51.5 %shard_map.100 = bf16[40,80,128]{2,1,0:T(8,128)(2,1)S(1)} custom-call(bf16[40,80,128]{2,1,0:T(8,128)(2,1)} %pair_in.1, s32[40,80]{1,0:T(8,128)} %mask_in.1, f32[1,128]{1,0:T(1,128)} %bitcast.4, f32[1,128]{1,0:T(1,128)} %bitcast.5, bf16[128,256]{1,0:T(8,128)(2,1)} %proj_w_in.1, bf16[128,256]{1,0:T(8,128)(2,1)} %gate_w_in.1, f32[1,128]{1,0:T(1,128)} %bitcast.6, ...), custom_call_target="tpu_custom_call" | custom-call | tf_op jit(solution)/shard_map/pallas_call | solution.py:385
  51.5 0.9 %copy.12 = bf16[40,80,128]{2,1,0:T(8,128)(2,1)} copy(bf16[40,80,128]{2,1,0:T(8,128)(2,1)S(1)} %shard_map.100) | data formatting | bytes 1638400
